TPU v7x, 512 devices: a whole 4x8x8 slice. The times are simulated.
512 devices in a mesh: dp: 8 (over x, core), seq: 64 (over y, z).
Axes of the slice: x: 4, y: 8, z: 8, core: 2. Of those that a mesh axis runs over, the one named last changes fastest.
Arguments:
- queries: bfloat16 [8, 8192, 1024], P('dp', 'seq'), may hold values from -6 to 6
- keys: bfloat16 [8, 8192, 1024], P('dp', 'seq'), may hold values from -6 to 6
- values: bfloat16 [8, 8192, 1024], P('dp', 'seq'), may hold values from -6 to 6
- cotangent: bfloat16 [8, 8192, 1024], P('dp', 'seq'), may hold values from -6 to 6
- out_weight: bfloat16 [1024, 1024], P('dp'), may hold values from -0.1875 to 0.1875
Outputs:
- output: bfloat16 [8, 8192, 1024], P('dp', 'seq')
- grad_queries: bfloat16 [8, 8192, 1024], P('dp', 'seq')
- grad_keys: bfloat16 [8, 8192, 1024], P('dp', 'seq')
- grad_values: bfloat16 [8, 8192, 1024], P('dp', 'seq')
- grad_weight: float32 [1024, 1024], P(('dp', 'seq'))
All inputs are finite; a program needn't handle non-finite values.
Results may differ from a plain program's by a relative error of at most 0.015.
Values may be sent and summed in bfloat16 or wider, within the bound.
A program may use at most 128 MiB of HBM per device.

v0:
```python
import math

import jax
import jax.numpy as jnp
from jax import lax
from jax.sharding import PartitionSpec as P

DH = 128


epsilon = 1e-05


def entering(x, axis, join, neutral, backward):
    count = lax.axis_size(axis)
    place = lax.axis_index(axis)
    ahead = count - 1 - place if backward else place
    gathered = lax.all_gather(x.astype(jnp.bfloat16), axis)
    state = jnp.zeros_like(x) + jnp.asarray(neutral, x.dtype)

    def one(turn, state):
        source = count - 1 - turn if backward else turn
        return join(state, lax.dynamic_index_in_dim(gathered, source, 0, False).astype(x.dtype))

    return lax.fori_loop(0, ahead, one, state)


def adding(earlier, latter):
    return earlier + latter


def contract_rows(left, right):
    return lax.dot_general(
        left, right, (((0,), (0,)), ((), ())), preferred_element_type=jnp.float32
    )


def apply_state(form, rows, state):
    upper = state.astype(jnp.bfloat16)
    lower = (state - upper.astype(jnp.float32)).astype(jnp.bfloat16)
    first = jnp.einsum(form, rows, upper, preferred_element_type=jnp.float32)
    return first + jnp.einsum(form, rows, lower, preferred_element_type=jnp.float32)


def local(queries, keys, values, cotangent, out_weight):
    local_seqs, block, features = queries.shape
    heads = features // DH
    shape = (local_seqs, block, heads, DH)
    query_heads = queries.reshape(shape)
    key_heads = keys.reshape(shape)
    value_heads = values.reshape(shape)
    causal = jnp.tril(jnp.ones((block, block), dtype=jnp.bool_))
    scores = jnp.einsum(
        "bthd,bshd->bhts", query_heads, key_heads, preferred_element_type=jnp.float32
    )
    attend = jnp.where(causal, scores, jnp.float32(0.0)).astype(jnp.bfloat16)
    local_kv = jnp.einsum(
        "bshd,bshe->bhde", key_heads, value_heads, preferred_element_type=jnp.float32
    )
    prior = entering(local_kv, "seq", adding, jnp.zeros_like(local_kv), False)
    mixed = jnp.einsum("bhts,bshd->bthd", attend, value_heads, preferred_element_type=jnp.float32)
    mixed = mixed + apply_state("bthd,bhde->bthe", query_heads, prior)
    root_mean = jnp.sqrt(jnp.mean(mixed * mixed, axis=-1, keepdims=True) + epsilon)
    normed = mixed / root_mean
    total_rows = local_seqs * block
    normed_rows = normed.astype(jnp.bfloat16).reshape(total_rows, features)
    out_rows = cotangent.reshape(total_rows, cotangent.shape[2])
    projected = lax.dot_general(
        normed_rows,
        lax.all_gather(out_weight, "dp", axis=0, tiled=True),
        (((1,), (1,)), ((), ())),
        preferred_element_type=jnp.float32,
    )
    columns = out_rows
    dnormed = jnp.dot(
        columns,
        lax.all_gather(out_weight, "dp", axis=0, tiled=True),
        preferred_element_type=jnp.float32,
    )
    output = projected.astype(jnp.bfloat16).reshape(local_seqs, block, cotangent.shape[2])
    dnormed = dnormed.reshape(shape)
    dmixed = (dnormed - normed * jnp.mean(dnormed * normed, axis=-1, keepdims=True)) / root_mean
    dmixed_b = dmixed.astype(jnp.bfloat16)
    local_u = jnp.einsum(
        "bthd,bthe->bhde", query_heads, dmixed_b, preferred_element_type=jnp.float32
    )
    later = entering(local_u, "seq", adding, jnp.zeros_like(local_u), True)
    back = jnp.where(
        causal,
        jnp.einsum("bthe,bshe->bhts", dmixed_b, value_heads, preferred_element_type=jnp.float32),
        jnp.float32(0.0),
    ).astype(jnp.bfloat16)
    grad_q = jnp.einsum("bhts,bshd->bthd", back, key_heads, preferred_element_type=jnp.float32)
    grad_q = grad_q + apply_state("bthe,bhde->bthd", dmixed_b, prior)
    grad_k = jnp.einsum("bhts,bthd->bshd", back, query_heads, preferred_element_type=jnp.float32)
    grad_k = grad_k + apply_state("bshe,bhde->bshd", value_heads, later)
    grad_v = jnp.einsum("bhts,bthe->bshe", attend, dmixed_b, preferred_element_type=jnp.float32)
    grad_v = grad_v + apply_state("bshd,bhde->bshe", key_heads, later)
    data_size = lax.axis_size("dp")
    seq_size = lax.axis_size("seq")
    factor = 1.0 / math.sqrt(local_seqs * data_size * block * seq_size)
    columns = out_rows
    grad_weight = lax.psum_scatter(
        contract_rows(columns, normed_rows) * factor, ("dp", "seq"), scatter_dimension=0, tiled=True
    )
    return (
        output,
        grad_q.reshape(local_seqs, block, features).astype(jnp.bfloat16),
        grad_k.reshape(local_seqs, block, features).astype(jnp.bfloat16),
        grad_v.reshape(local_seqs, block, features).astype(jnp.bfloat16),
        grad_weight,
    )


def solution(mesh):
    return jax.shard_map(
        local,
        mesh=mesh,
        in_specs=(
            P("dp", "seq", None),
            P("dp", "seq", None),
            P("dp", "seq", None),
            P("dp", "seq", None),
            P("dp", None),
        ),
        out_specs=(
            P("dp", "seq", None),
            P("dp", "seq", None),
            P("dp", "seq", None),
            P("dp", "seq", None),
            P(("dp", "seq"), None),
        ),
        check_vma=False,
    )
```

profile of v0, /device:TPU:1, one launch (start us, length us, event | category | flops | bytes accessed | tf_op | source)
XLA Modules:
  0.0 763.9 jit_solution(2272263269499329153)
XLA Ops:
  9.2 1.1 copy.80
  13.4 33.2 %all-gather.6.cloned.1.call-done = bf16[1024,1024]{1,0:T(8,128)(2,1)} async-done(((bf16[128,1024]{1,0:T(8,128)(2,1)}), bf16[1024,1024]{1,0:T(8,128)(2,1)}) %all-gather.6.cloned.1.call-update) | async-done | bytes 2097168 | tf_op jit(solution)/shard_map/all_gather | solution.py:70
  46.6 2.9 copy.49
  49.4 140.7 %all-gather.8.cloned.1.call-done = bf16[512,128,128]{2,1,0:T(8,128)(2,1)} async-done(((bf16[8,128,128]{2,1,0:T(8,128)(2,1)}), bf16[512,128,128]{2,1,0:T(8,128)(2,1)}) %all-gather.8.cloned.1.call-update) | async-done | bytes 16777232 | tf_op jit(solution)/shard_map/all_gather | solution.py:18
  190.9 1.3 multiply_reduce_fusion.1
  194.5 2.7 multiply_bitcast_fusion
  197.2 2.0 fusion.11
  199.2 1.8 copy.57
  201.0 1.3 fusion.7
  202.3 1.3 fusion.22
  203.6 1.2 convolution_add_fusion.2
  204.8 1.3 fusion.9
  206.9 2.5 fusion.10
  209.4 1.2 fusion.18
  210.6 335.2 %all-reduce.3.cloned.1.call-done = f32[1024,1024]{0,1:T(8,128)} async-done(((f32[1024,1024]{0,1:T(8,128)}), f32[1024,1024]{0,1:T(8,128)}) %all-reduce.3.cloned.1.call-update) | async-done | bytes 4194320
  545.8 1.2 constant_dynamic-slice_fusion
  547.9 137.3 %all-gather.10.cloned.1.call-done = bf16[512,128,128]{2,1,0:T(8,128)(2,1)} async-done(((bf16[8,128,128]{2,1,0:T(8,128)(2,1)}), bf16[512,128,128]{2,1,0:T(8,128)(2,1)}) %all-gather.10.cloned.1.call-update) | async-done | bytes 16777232 | tf_op jit(solution)/shard_map/all_gather | solution.py:18
  685.2 68.9 %while.23 = (s32[]{:T(128)}, f32[1,8,128,128]{3,2,1,0:T(8,128)S(1)}, s32[]{:T(128)}, bf16[64,1,8,128,128]{4,3,2,1,0:T(8,128)(2,1)}, s32[]{:T(128)}, /*index=5*/s32[]{:T(128)}, s32[]{:T(128)}, s32[]{:T(128)}) while((s32[]{:T(128)}, f32[1,8,128,128]{3,2,1,0:T(8,128)S(1)}, s32[]{:T(128)}, bf16[64,1,8,128,128]{4,3,2,1,0:T(8,128)(2,1)}, s32[]{:T(128)}, ...), condition=%wide.region_5.6_spmd, body=%wide.region_4.5_spmd.sunk | while | flops 262150 | bytes 1310863 | solution.py:25
  685.3 1.1 convert_add_fusion.5
  686.4 1.1 convert_add_fusion.5
  688.6 1.1 convert_add_fusion.5
  689.7 1.1 convert_add_fusion.5
  690.8 1.1 convert_add_fusion.5
  692.9 1.1 convert_add_fusion.5
  694.0 1.1 convert_add_fusion.5
  695.1 1.1 convert_add_fusion.5
  697.3 1.1 convert_add_fusion.5
  698.4 1.1 convert_add_fusion.5
  699.5 1.1 convert_add_fusion.5
  701.7 1.1 convert_add_fusion.5
  702.8 1.1 convert_add_fusion.5
  706.1 1.1 convert_add_fusion.5
  (99 shorter events, 65.4 us)
Async XLA Ops:
  7.2 185.0 %copy-start = (bf16[1,128,1024]{2,1,0:T(8,128)(2,1)S(1)}, bf16[1,128,1024]{2,1,0:T(8,128)(2,1)}, u32[]{:S(2)}) copy-start(bf16[1,128,1024]{2,1,0:T(8,128)(2,1)} %param.12) | copy-start | bytes 786436
  7.2 39.4 %all-gather.6.cloned.1.call-start = ((), (), s32[]{:S(2)}) async-start(), calls=%async_computation | async-start | bytes 2359296 | tf_op jit(solution)/shard_map/all_gather | solution.py:70
  7.9 182.2 %all-gather.8.cloned.1.call-start = ((), (), s32[]{:S(2)}) async-start(), calls=%async_computation.1 | async-start | bytes 17039360 | tf_op jit(solution)/shard_map/all_gather | solution.py:18
  9.0 181.2 %copy-start.3 = (bf16[16,8,8,128]{3,2,1,0:T(8,128)(2,1)}, bf16[16,8,8,128]{3,2,1,0:T(8,128)(2,1)S(1)}, u32[]{:S(2)}) copy-start(bf16[16,8,8,128]{3,2,1,0:T(8,128)(2,1)S(1)} %copy.79) | copy-start | bytes 786436
  9.2 2.1 copy-start.5
  11.3 534.6 %all-reduce.3.cloned.1.call-start = ((), (), s32[]{:S(2)}) async-start(), calls=%async_computation.3 | async-start | bytes 8388608
  193.8 0.7 copy-start.6
  197.2 9.8 %copy-start.1 = (bf16[1024,1024]{1,0:T(8,128)(2,1)S(1)}, bf16[1024,1024]{1,0:T(8,128)(2,1)}, u32[]{:S(2)}) copy-start(bf16[1024,1024]{1,0:T(8,128)(2,1)} %all-gather.6.cloned.1.call-done) | copy-start | bytes 6291460
  197.2 488.0 %all-gather.10.cloned.1.call-start = ((), (), s32[]{:S(2)}) async-start(), calls=%async_computation.2 | async-start | bytes 17039360 | tf_op jit(solution)/shard_map/all_gather | solution.py:18
  202.3 3.8 copy-start.7
  204.8 4.7 copy-start.2
  685.2 69.2 %copy-start.4 = (bf16[16,8,8,128]{3,2,1,0:T(8,128)(2,1)S(1)}, bf16[16,8,8,128]{3,2,1,0:T(8,128)(2,1)}, u32[]{:S(2)}) copy-start(bf16[16,8,8,128]{3,2,1,0:T(8,128)(2,1)} %copy-done.3) | copy-start | bytes 786436
  685.2 69.8 %copy-start.8 = (bf16[8,128,128]{2,1,0:T(8,128)(2,1)S(1)}, bf16[8,128,128]{2,1,0:T(8,128)(2,1)}, u32[]{:S(2)}) copy-start(bf16[8,128,128]{2,1,0:T(8,128)(2,1)} %copy-done.7) | copy-start | bytes 786436
Sparse Core Ops, SparseCore 0:
  10.2 36.3 all-gather.5
  50.2 139.9 all-gather.7
  197.3 348.5 all-reduce.2
  548.7 136.4 all-gather.9
where the time goes:
time: 766 us; the launch traced here: 764 us
  waiting for transfers between devices  647 us (84%)
  other arithmetic  68.3 us (9%)
  matrix products  19.5 us (3%)
  between operations  14 us (2%)
  local copies, waits for them, and re-layouts  13.3 us (2%)
    unnamed x5, waiting for transfers between devices  336 us
    all_gather x2, waiting for transfers between devices, entering(): gathered = lax.all_gather(x.astype(jnp.bfloat16), axis)  278 us
    add x63, other arithmetic, adding(): return earlier + latter  67.4 us
    all_gather x1, waiting for transfers between devices, local(): lax.all_gather(out_weight, 'dp', axis=0, tiled=True)  33.2 us
  transfers between devices with their start and end apart: 4, of which 4 were waited for; matrix products, arithmetic and copies ran while one was open for 3% of the time, Pallas kernels for 0%

commit v1 on v0

v1 whole, which is shorter than its diff:
```python
import functools
import math

import jax
import jax.numpy as jnp
from jax import lax
from jax.experimental import pallas as pl
from jax.experimental.pallas import tpu as pltpu
from jax.sharding import PartitionSpec as P

MESH = pl.DeviceIdType.MESH
DH = 128
EPSILON = 1e-05
BF16 = jnp.bfloat16
F32 = jnp.float32


def dot(left, right, contract):
    return lax.dot_general(left, right, ((contract[:1], contract[1:]), ((), ())), preferred_element_type=F32)


def head_cols(h):
    return pl.ds(pl.multiple_of(h * DH, DH), DH)


def kernel(
    sizes,
    q_hbm, k_hbm, v_hbm, c_hbm, w_hbm,
    out_hbm, gq_hbm, gk_hbm, gv_hbm, gw_hbm,
    q, k, v, c, wall, dn,
    a_send, a_recv, p_send, prior,
    b_send, b_recv, l_send, later,
    attend, part, normed, dmixed, nall, ccol, ccolt,
    gk_part, gv_part, g_tile, g_rows, g_send, g_recv,
    out_v, gq_v, gk_v, gv_v, gw_v,
    load_sem, store_sem, send_sem, a_sem, p_sem, b_sem, l_sem, g_sem,
    w_sem, c_sem, n_sem,
):
    dps, ny, nz, heads = sizes
    nx = dps // 2
    seqs = ny * nz
    block = q.shape[0]
    me_dp, me = lax.axis_index("dp"), lax.axis_index("seq")
    x, core = me_dp // 2, me_dp % 2
    y, z = me // nz, me % nz
    right = ((x + 1) % nx) * 2 + core
    left = ((x + nx - 1) % nx) * 2 + core
    sibling = x * 2 + (1 - core)
    opposite = ((x + 2) % nx) * 2 + core
    right_s = ((x + 1) % nx) * 2 + (1 - core)
    left_s = ((x + nx - 1) % nx) * 2 + (1 - core)
    opposite_s = ((x + 2) % nx) * 2 + (1 - core)

    def turn(i):
        return (ny + (2 * (i % 2) - 1) * ((i + 1) // 2)) % ny

    barrier = pltpu.get_barrier_semaphore()

    def greet_seq(i, carry):
        pl.semaphore_signal(barrier, inc=1, device_id=(me_dp, (me + i) % seqs), device_id_type=MESH)
        return carry

    def greet_dp(i, carry):
        pl.semaphore_signal(barrier, inc=1, device_id=((me_dp + i) % dps, me), device_id_type=MESH)
        return carry

    loads = [
        pltpu.make_async_copy(src, dst, load_sem.at[i])
        for i, (src, dst) in enumerate(
            [(k_hbm, k), (v_hbm, v), (w_hbm, wall.at[me_dp]), (c_hbm, c), (q_hbm, q)]
        )
    ]
    for load in loads:
        load.start()
    lax.fori_loop(1, seqs, greet_seq, 0)
    lax.fori_loop(1, dps, greet_dp, 0)

    loads[0].wait()
    loads[1].wait()

    def local_state(h, carry):
        kv = dot(k[:, head_cols(h)], v[:, head_cols(h)], (0, 0))
        a_send[pl.ds(h * 8, 8)] = kv.astype(BF16).reshape(8, 16, DH)
        return carry

    lax.fori_loop(0, heads, local_state, 0)
    a_recv[me] = a_send[me]
    loads[2].wait()
    pl.semaphore_wait(barrier, seqs - 1 + dps - 1)

    def remote(src, dst, send, recv, dp, seq):
        return pltpu.make_async_remote_copy(
            src_ref=src, dst_ref=dst, send_sem=send, recv_sem=recv, device_id=(dp, seq), device_id_type=MESH
        )

    def arrived(ref, sem):
        remote(ref, ref, send_sem.at[0], sem, sibling, me).wait_recv()

    W_LEFT, W_RIGHT, W_OPP0, W_OPP1, W_SIB, W_SIB_LEFT, W_SIB_RIGHT, W_SIB_OPP = range(8)
    half = block // 2
    own_w = wall.at[me_dp]
    remote(own_w, own_w, send_sem.at[0], w_sem.at[W_LEFT], right, me).start()
    remote(own_w, own_w, send_sem.at[0], w_sem.at[W_RIGHT], left, me).start()
    remote(own_w, own_w, send_sem.at[0], w_sem.at[W_SIB], sibling, me).start()

    def scatter(source, landing, send, recv):
        def one(i, carry):
            target = ((y + turn(i // nz)) % ny) * nz + (z + i) % nz
            remote(source.at[target], landing.at[me], send, recv, me_dp, target).start()
            return carry

        lax.fori_loop(1, seqs, one, 0)

    scatter(a_send, a_recv, send_sem.at[1], a_sem)

    loads[3].wait()
    ccol[me_dp] = c[:, head_cols(me_dp)]

    def send_columns(i, carry):
        target = (me_dp + i) % dps
        remote(c.at[:, head_cols(target)], ccol.at[me_dp], send_sem.at[2], c_sem, target, me).start()
        return carry

    lax.fori_loop(1, dps, send_columns, 0)

    loads[4].wait()
    causal = lax.broadcasted_iota(jnp.int32, (block, block), 0) >= lax.broadcasted_iota(
        jnp.int32, (block, block), 1
    )

    def within(h, carry):
        scores = dot(q[:, head_cols(h)], k[:, head_cols(h)], (1, 1))
        near = jnp.where(causal, scores, 0.0).astype(BF16)
        attend[h] = near
        part[h] = dot(near, v[:, head_cols(h)], (1, 0))
        return carry

    lax.fori_loop(0, heads, within, 0)

    arrived(a_recv.at[pl.ds(0, seqs - 1)], a_sem)

    def forward_sum(s, total):
        p_send[s] = total.astype(BF16)
        return total + a_recv[s].astype(F32)

    lax.fori_loop(0, seqs, forward_sum, jnp.zeros((16, DH), F32))
    prior[me] = p_send[me]

    def give_back(source, landing, send, recv):
        def one(i, carry):
            target = ((y + turn(i // nz)) % ny) * nz + (z + i) % nz
            remote(source.at[target], landing.at[me], send, recv.at[y], me_dp, target).start()
            return carry

        lax.fori_loop(1, seqs, one, 0)

    give_back(p_send, prior, send_sem.at[3], p_sem)

    from_left, from_right = wall.at[left], wall.at[right]
    arrived(from_left, w_sem.at[W_LEFT])
    low, high = pl.ds(0, half), pl.ds(half, half)
    remote(from_left.at[low], from_left.at[low], send_sem.at[0], w_sem.at[W_OPP0], right, me).start()
    remote(from_left, from_left, send_sem.at[0], w_sem.at[W_SIB_LEFT], sibling, me).start()
    arrived(from_right, w_sem.at[W_RIGHT])
    remote(from_right.at[high], from_right.at[high], send_sem.at[0], w_sem.at[W_OPP1], left, me).start()
    remote(from_right, from_right, send_sem.at[0], w_sem.at[W_SIB_RIGHT], sibling, me).start()

    dn[...] = jnp.zeros_like(dn)

    def add_rows(d):
        dn[...] += dot(c[:, head_cols(d)], wall[d], (1, 0))

    add_rows(me_dp)
    add_rows(left)
    add_rows(right)
    arrived(wall.at[sibling], w_sem.at[W_SIB])
    add_rows(sibling)
    arrived(wall.at[opposite, low], w_sem.at[W_OPP0])
    arrived(wall.at[opposite, high], w_sem.at[W_OPP1])
    remote(wall.at[opposite], wall.at[opposite], send_sem.at[0], w_sem.at[W_SIB_OPP], sibling, me).start()
    add_rows(opposite)
    arrived(wall.at[left_s], w_sem.at[W_SIB_LEFT])
    add_rows(left_s)
    arrived(wall.at[right_s], w_sem.at[W_SIB_RIGHT])
    add_rows(right_s)
    arrived(wall.at[opposite_s], w_sem.at[W_SIB_OPP])
    add_rows(opposite_s)

    N_LEFT, N_RIGHT, N_OPP0, N_OPP1, N_SIB, N_SIB_LEFT, N_SIB_RIGHT, N_SIB_OPP = range(8)

    def middle(h, first):
        mixed = part[h] + dot(q[:, head_cols(h)], prior[pl.ds(h * 8, 8)].reshape(DH, DH), (1, 0))
        inverse = lax.rsqrt(jnp.mean(mixed * mixed, axis=-1, keepdims=True) + EPSILON)
        n = mixed * inverse
        dnormed = dn[:, head_cols(h)]
        dmix = (dnormed - n * jnp.mean(dnormed * n, axis=-1, keepdims=True)) * inverse
        dmix = dmix.astype(BF16)
        u = dot(q[:, head_cols(h)], dmix, (0, 0))
        b_send[pl.ds(h * 8, 8)] = u.astype(BF16).reshape(8, 16, DH)
        dmixed[h] = dmix
        n = n.astype(BF16)
        nall[h, me_dp] = n
        normed[:, head_cols(h)] = n

        def one(i, carry):
            target = h * nz + (z + i) % nz
            remote(b_send.at[target], b_recv.at[me], send_sem.at[4], b_sem, me_dp, target).start()
            return carry

        lax.fori_loop(1 if first else 0, nz, one, 0)
        own_n = nall.at[h, me_dp]
        remote(own_n, own_n, send_sem.at[5], n_sem.at[N_LEFT], right, me).start()
        remote(own_n, own_n, send_sem.at[5], n_sem.at[N_RIGHT], left, me).start()
        remote(own_n, own_n, send_sem.at[5], n_sem.at[N_SIB], sibling, me).start()

    arrived(prior.at[pl.ds(0, nz - 1)], p_sem.at[y])
    middle(y, True)
    b_recv[me] = b_send[me]

    def other_heads(i, carry):
        h = (y + ny - turn(i)) % ny
        arrived(prior.at[pl.ds(h * 8, 8)], p_sem.at[h])
        middle(h, False)
        return carry

    lax.fori_loop(1, heads, other_heads, 0)

    def within_back(h, carry):
        cols = head_cols(h)
        dmix = dmixed[h]
        back = jnp.where(causal, dot(dmix, v[:, cols], (1, 1)), 0.0).astype(BF16)
        grad_q = dot(back, k[:, cols], (1, 0)) + dot(dmix, prior[pl.ds(h * 8, 8)].reshape(DH, DH), (1, 1))
        gq_v[:, cols] = grad_q.astype(BF16)
        gk_part[h] = dot(back, q[:, cols], (0, 0))
        gv_part[h] = dot(attend[h], dmix, (0, 0))
        return carry

    lax.fori_loop(0, heads, within_back, 0)
    stores = [pltpu.make_async_copy(gq_v, gq_hbm, store_sem.at[0])]
    stores[0].start()

    arrived(b_recv.at[pl.ds(0, seqs - 1)], b_sem)

    def backward_sum(i, total):
        s = seqs - 1 - i
        l_send[s] = total.astype(BF16)
        return total + b_recv[s].astype(F32)

    lax.fori_loop(0, seqs, backward_sum, jnp.zeros((16, DH), F32))
    later[me] = l_send[me]
    give_back(l_send, later, send_sem.at[6], l_sem)

    lower, upper = pl.ds(0, heads // 2), pl.ds(heads // 2, heads // 2)

    def arrived_heads(who, sem, count=heads):
        remote(nall.at[0, pl.ds(0, count)], nall.at[0, pl.ds(0, count)], send_sem.at[0], sem, who, me).wait_recv()

    def pass_on(who, sem, to, first, count):
        def one(h, carry):
            there = nall.at[h, who]
            remote(there, there, send_sem.at[5], sem, to, me).start()
            return carry

        lax.fori_loop(first, first + count, one, 0)

    arrived_heads(left, n_sem.at[N_LEFT])
    pass_on(left, n_sem.at[N_OPP0], right, 0, heads // 2)
    pass_on(left, n_sem.at[N_SIB_LEFT], sibling, 0, heads)
    arrived_heads(right, n_sem.at[N_RIGHT])
    pass_on(right, n_sem.at[N_OPP1], left, heads // 2, heads // 2)
    pass_on(right, n_sem.at[N_SIB_RIGHT], sibling, 0, heads)

    def project(d, carry):
        out_v[:, head_cols(d)] = dot(normed[...], wall[d], (1, 1)).astype(BF16)
        return carry

    lax.fori_loop(0, dps, project, 0)
    stores.append(pltpu.make_async_copy(out_v, out_hbm, store_sem.at[1]))
    stores[1].start()

    arrived(ccol.at[pl.ds(0, dps - 1)], c_sem)

    def transpose(d, carry):
        ccolt[:, head_cols(d)] = ccol[d].T
        return carry

    lax.fori_loop(0, dps, transpose, 0)

    arrived_heads(opposite, n_sem.at[N_OPP0], heads // 2)
    arrived_heads(opposite, n_sem.at[N_OPP1], heads // 2)
    pass_on(opposite, n_sem.at[N_SIB_OPP], sibling, 0, heads)
    arrived_heads(sibling, n_sem.at[N_SIB])
    arrived_heads(left_s, n_sem.at[N_SIB_LEFT])
    arrived_heads(right_s, n_sem.at[N_SIB_RIGHT])
    arrived_heads(opposite_s, n_sem.at[N_SIB_OPP])

    factor = 1.0 / math.sqrt(dps * block * seqs)

    def weight_rows(h, carry):
        g_tile[...] = dot(ccolt[...], nall[h].reshape(dps * block, DH), (1, 0)) * factor
        for r in range(2):
            g_rows[pl.ds(2 * h + r, seqs, stride=16), :] = g_tile[pl.ds(r, seqs, stride=2), :]
        return carry

    lax.fori_loop(0, heads, weight_rows, 0)

    def round_rows(s, carry):
        g_send[s] = g_rows[pl.ds(pl.multiple_of(s * 16, 16), 16), :].astype(BF16)
        return carry

    lax.fori_loop(0, seqs, round_rows, 0)
    g_recv[me] = g_send[me]
    scatter(g_send, g_recv, send_sem.at[7], g_sem)

    def finish(h):
        cols = head_cols(h)
        state = later[pl.ds(h * 8, 8)].reshape(DH, DH)
        gk_v[:, cols] = (gk_part[h] + dot(v[:, cols], state, (1, 1))).astype(BF16)
        gv_v[:, cols] = (gv_part[h] + dot(k[:, cols], state, (1, 0))).astype(BF16)

    arrived(later.at[pl.ds(0, nz - 1)], l_sem.at[y])
    finish(y)

    def finish_others(i, carry):
        h = (y + ny - turn(i)) % ny
        arrived(later.at[pl.ds(h * 8, 8)], l_sem.at[h])
        finish(h)
        return carry

    lax.fori_loop(1, heads, finish_others, 0)
    stores.append(pltpu.make_async_copy(gk_v, gk_hbm, store_sem.at[2]))
    stores.append(pltpu.make_async_copy(gv_v, gv_hbm, store_sem.at[3]))
    stores[2].start()
    stores[3].start()

    arrived(g_recv.at[pl.ds(0, seqs - 1)], g_sem)
    total = lax.fori_loop(0, seqs, lambda s, t: t + g_recv[s].astype(F32), jnp.zeros((16, DH), F32))
    for h in range(heads):
        gw_v[:, h * DH : (h + 1) * DH] = total[2 * h : 2 * h + 2]
    stores.append(pltpu.make_async_copy(gw_v, gw_hbm, store_sem.at[4]))
    stores[4].start()

    def sent(ref, i):
        remote(ref, ref, send_sem.at[i], a_sem, sibling, me).wait_send()

    sent(wall.at[pl.ds(0, 7)], 0)
    sent(a_send.at[pl.ds(0, seqs - 1)], 1)
    sent(ccol.at[pl.ds(0, dps - 1)], 2)
    sent(p_send.at[pl.ds(0, seqs - 1)], 3)
    sent(b_send.at[pl.ds(0, seqs - 1)], 4)
    sent(nall.at[pl.ds(0, 7)], 5)
    sent(l_send.at[pl.ds(0, seqs - 1)], 6)
    sent(g_send.at[pl.ds(0, seqs - 1)], 7)
    for store in stores:
        store.wait()


def local(sizes, queries, keys, values, cotangent, out_weight):
    dps, ny, nz, heads = sizes
    _, block, features = queries.shape
    seqs = ny * nz
    rows = jax.ShapeDtypeStruct((block, features), BF16)
    states = pltpu.VMEM((seqs, 16, DH), BF16)
    whole = pltpu.VMEM((block, features), BF16)
    per_head = pltpu.VMEM((heads, block, DH), F32)
    dma = pltpu.SemaphoreType.DMA
    out = pl.pallas_call(
        functools.partial(kernel, sizes),
        out_shape=[rows] * 4 + [jax.ShapeDtypeStruct((2, features), F32)],
        in_specs=[pl.BlockSpec(memory_space=pl.ANY)] * 5,
        out_specs=[pl.BlockSpec(memory_space=pl.ANY)] * 5,
        scratch_shapes=[
            whole, whole, whole, whole,
            pltpu.VMEM((dps, block, features), BF16),
            pltpu.VMEM((block, features), F32),
            states, states, states, states,
            states, states, states, states,
            pltpu.VMEM((heads, block, block), BF16),
            per_head,
            whole,
            pltpu.VMEM((heads, block, DH), BF16),
            pltpu.VMEM((heads, dps, block, DH), BF16),
            pltpu.VMEM((dps, block, DH), BF16),
            pltpu.VMEM((DH, dps * block), BF16),
            per_head, per_head,
            pltpu.VMEM((block, DH), F32),
            pltpu.VMEM((seqs * 16, DH), F32),
            states, states,
            whole, whole, whole, whole,
            pltpu.VMEM((2, features), F32),
            dma((5,)), dma((5,)), dma((8,)), dma, dma((heads,)), dma, dma((heads,)), dma,
            dma((8,)), dma, dma((8,)),
        ],
        compiler_params=pltpu.CompilerParams(
            collective_id=0, has_side_effects=True, vmem_limit_bytes=40 * 1024 * 1024
        ),
    )(queries[0], keys[0], values[0], cotangent[0], out_weight)
    return tuple(part[None] for part in out[:4]) + (out[4],)


def solution(mesh):
    seqs = mesh.shape["seq"]
    ny = nz = math.isqrt(seqs)
    sizes = (mesh.shape["dp"], ny, nz, 8)
    tokens = P("dp", "seq", None)
    return jax.shard_map(
        functools.partial(local, sizes),
        mesh=mesh,
        in_specs=(tokens, tokens, tokens, tokens, P("dp", None)),
        out_specs=(tokens, tokens, tokens, tokens, P(("dp", "seq"), None)),
        check_vma=False,
    )
```

time: 766 us -> 82.5 us (0.11)
  waiting for transfers between devices: 647 us -> 0 us
  Pallas kernels: 0 us -> 73.4 us
  other arithmetic: 68.3 us -> 0 us
  matrix products: 19.5 us -> 0 us
  between operations: 14 us -> 0.66 us
    unnamed x5 -> x0, waiting for transfers between devices: 336 us -> none
    all_gather x3 -> x0, waiting for transfers between devices: 311 us -> none  [the longest x2 278 us: entering(): gathered = lax.all_gather(x.astype(jnp.bfloat16), axis)]
    pallas_call x0 -> x1, Pallas kernels: none -> 73.4 us  [local(): pl.pallas_call(functools.partial(kernel, sizes), out_shape=[rows] * 4 + [...]
    add x63 -> x0, other arithmetic: 67.4 us -> none  [adding(): return earlier + latter]
    dot_general x19 -> x0, matrix products: 19.5 us -> none  [the longest x1 2.66 us: contract_rows(): lax.dot_general(left, right, (((0,), (0,)), ((), ())), preferred_element_...]
  transfers between devices with their start and end apart: 4 -> 0, of which waited for: 4 -> 0; matrix products, arithmetic and copies ran while one was open for 3% -> 0% of each run, Pallas kernels for 0% -> 0%
where the time goes in v1:
time: 82.5 us; the launch traced here: 82.2 us
  Pallas kernels  73.4 us (89%)
  local copies, waits for them, and re-layouts  8.15 us (10%)
    pallas_call x1, Pallas kernels, local(): pl.pallas_call(functools.partial(kernel, sizes), out_shape=[rows] * 4 + [...  73.4 us
    unnamed x15, local copies, waits for them, and re-layouts  8.15 us

profile of v1, /device:TPU:1, one launch (start us, length us, event | category | flops | bytes accessed | tf_op | source)
XLA Modules:
  0.0 82.2 jit_solution(2041712166891364010)
XLA Ops:
  0.6 0.0 copy-start
  0.6 0.9 %copy-done = bf16[1,128,1024]{2,1,0:T(8,128)(2,1)S(1)} copy-done((bf16[1,128,1024]{2,1,0:T(8,128)(2,1)S(1)}, bf16[1,128,1024]{2,1,0:T(8,128)(2,1)}, u32[]{:S(2)}) %copy-start) | copy-done | bytes 262168
  1.6 0.0 copy-start.1
  1.6 0.9 %copy-done.1 = bf16[1,128,1024]{2,1,0:T(8,128)(2,1)S(1)} copy-done((bf16[1,128,1024]{2,1,0:T(8,128)(2,1)S(1)}, bf16[1,128,1024]{2,1,0:T(8,128)(2,1)}, u32[]{:S(2)}) %copy-start.1) | copy-done | bytes 262168
  2.5 0.0 copy-start.2
  2.5 0.9 %copy-done.2 = bf16[1,128,1024]{2,1,0:T(8,128)(2,1)S(1)} copy-done((bf16[1,128,1024]{2,1,0:T(8,128)(2,1)S(1)}, bf16[1,128,1024]{2,1,0:T(8,128)(2,1)}, u32[]{:S(2)}) %copy-start.2) | copy-done | bytes 262168
  3.5 0.0 copy-start.3
  3.5 0.9 %copy-done.3 = bf16[1,128,1024]{2,1,0:T(8,128)(2,1)S(1)} copy-done((bf16[1,128,1024]{2,1,0:T(8,128)(2,1)S(1)}, bf16[1,128,1024]{2,1,0:T(8,128)(2,1)}, u32[]{:S(2)}) %copy-start.3) | copy-done | bytes 262168
  4.4 0.0 copy-start.4
  4.4 0.9 %copy-done.4 = bf16[128,1024]{1,0:T(8,128)(2,1)S(1)} copy-done((bf16[128,1024]{1,0:T(8,128)(2,1)S(1)}, bf16[128,1024]{1,0:T(8,128)(2,1)}, u32[]{:S(2)}) %copy-start.4) | copy-done | bytes 262168
  5.4 73.4 %shard_map.92 = (bf16[128,1024]{1,0:T(8,128)(2,1)S(1)}, bf16[128,1024]{1,0:T(8,128)(2,1)S(1)}, bf16[128,1024]{1,0:T(8,128)(2,1)S(1)}, bf16[128,1024]{1,0:T(8,128)(2,1)S(1)}, f32[2,1024]{1,0:T(2,128)S(1)}) custom-call(bf16[128,1024]{1,0:T(8,128)(2,1)S(1)} %bitcast.8, bf16[128,1024]{1,0:T(8,128)(2,1)S(1)} %bitcast.9, bf16[128,1024]{1,0:T(8,128)(2,1)S(1)} %bitcast.10, ...), custom_call_target="tpu_custom_call" | custom-call | tf_op jit(solution)/shard_map/pallas_call | solution.py:367
  78.8 0.7 copy.15
  79.5 0.7 copy.16
  80.2 0.7 copy.17
  80.9 0.7 copy.18
  81.6 0.6 copy.19
Async XLA Ops:
  0.6 1.0 %copy-start = (bf16[1,128,1024]{2,1,0:T(8,128)(2,1)S(1)}, bf16[1,128,1024]{2,1,0:T(8,128)(2,1)}, u32[]{:S(2)}) copy-start(bf16[1,128,1024]{2,1,0:T(8,128)(2,1)} %param.5) | copy-start | bytes 786436
  1.6 0.9 %copy-start.1 = (bf16[1,128,1024]{2,1,0:T(8,128)(2,1)S(1)}, bf16[1,128,1024]{2,1,0:T(8,128)(2,1)}, u32[]{:S(2)}) copy-start(bf16[1,128,1024]{2,1,0:T(8,128)(2,1)} %param.6) | copy-start | bytes 786436
  2.5 0.9 %copy-start.2 = (bf16[1,128,1024]{2,1,0:T(8,128)(2,1)S(1)}, bf16[1,128,1024]{2,1,0:T(8,128)(2,1)}, u32[]{:S(2)}) copy-start(bf16[1,128,1024]{2,1,0:T(8,128)(2,1)} %param.7) | copy-start | bytes 786436
  3.5 0.9 %copy-start.3 = (bf16[1,128,1024]{2,1,0:T(8,128)(2,1)S(1)}, bf16[1,128,1024]{2,1,0:T(8,128)(2,1)}, u32[]{:S(2)}) copy-start(bf16[1,128,1024]{2,1,0:T(8,128)(2,1)} %param.8) | copy-start | bytes 786436
  4.4 0.9 %copy-start.4 = (bf16[128,1024]{1,0:T(8,128)(2,1)S(1)}, bf16[128,1024]{1,0:T(8,128)(2,1)}, u32[]{:S(2)}) copy-start(bf16[128,1024]{1,0:T(8,128)(2,1)} %w_hbm.1) | copy-start | bytes 786436

commit v2 on v1

v2 whole, which is shorter than its diff:
```python
import functools
import math

import jax
import jax.numpy as jnp
from jax import lax
from jax.experimental import pallas as pl
from jax.experimental.pallas import tpu as pltpu
from jax.sharding import PartitionSpec as P

MESH = pl.DeviceIdType.MESH
DH = 128
EPSILON = 1e-05
BF16 = jnp.bfloat16
F32 = jnp.float32
VMEM_LIMIT = 40 * 1024 * 1024


def dot(left, right, contract):
    return lax.dot_general(left, right, ((contract[:1], contract[1:]), ((), ())), preferred_element_type=F32)


def head_cols(h):
    return pl.ds(pl.multiple_of(h * DH, DH), DH)


def far_first(count):
    return sorted(range(count), key=lambda d: -min(d, count - d))


def kernel(
    sizes,
    q_hbm, k_hbm, v_hbm, c_hbm, w_hbm,
    out_hbm, gq_hbm, gk_hbm, gv_hbm, gw_hbm,
    q, k, v, c, wall, dn,
    a_send, a_recv, p_send, prior,
    b_send, b_recv, l_send, later,
    attend, part, normed, dmixed, n_send, nall, ccol, ccolt,
    gk_part, gv_part, g_tile, g_rows, g_send, g_recv, g_sum, g_other,
    out_v, gq_v, gk_v, gv_v, gw_v,
    load_sem, store_sem, send_sem, a_sem, p_sem, b_sem, l_sem, g_sem,
    w_sem, c_sem, n_sem, swap_sem,
):
    dps, ny, nz, heads = sizes
    nx = dps // 2
    seqs = ny * nz
    block = q.shape[0]
    half = block // 2
    me_dp, me = lax.axis_index("dp"), lax.axis_index("seq")
    x, core = me_dp // 2, me_dp % 2
    y, z = me // nz, me % nz
    x_right, x_left, x_opposite = (x + 1) % nx, (x + nx - 1) % nx, (x + 2) % nx
    other = 1 - core
    right, left, opposite = x_right * 2 + core, x_left * 2 + core, x_opposite * 2 + core
    sibling = x * 2 + other
    right_s, left_s, opposite_s = x_right * 2 + other, x_left * 2 + other, x_opposite * 2 + other

    y_order, z_order = far_first(ny), far_first(nz)
    columns = [(z + d) % nz for d in z_order]

    def row_at(i):
        step = (ny - i) // 2
        sign = 2 * (i % 2) - 1
        return (y + ny + sign * step) % ny

    def each_other(act):
        def rows(i, carry):
            base = row_at(i) * nz
            for column in columns:
                act(base + column)
            return carry

        lax.fori_loop(0, ny - 1, rows, 0)
        for column in columns[:-1]:
            act(y * nz + column)

    loads = [
        pltpu.make_async_copy(src, dst, load_sem.at[i])
        for i, (src, dst) in enumerate(
            [(k_hbm, k), (v_hbm, v), (w_hbm, wall.at[me_dp]), (q_hbm, q), (c_hbm, c)]
        )
    ]
    for load in loads:
        load.start()

    barrier = pltpu.get_barrier_semaphore()

    def greet(dp, seq):
        pl.semaphore_signal(barrier, inc=1, device_id=(dp, seq), device_id_type=MESH)

    each_other(lambda seq: greet(me_dp, seq))
    for dp in (opposite, opposite_s, right, left, right_s, left_s, sibling):
        greet(dp, me)

    loads[0].wait()
    loads[1].wait()
    for h in range(heads):
        cols = slice(h * DH, (h + 1) * DH)
        a_send[h * 8 : h * 8 + 8] = dot(k[:, cols], v[:, cols], (0, 0)).astype(BF16).reshape(8, 16, DH)
    a_recv[me] = a_send[me]
    loads[2].wait()
    pl.semaphore_wait(barrier, seqs - 1 + dps - 1)

    def remote(src, dst, send, recv, dp, seq):
        return pltpu.make_async_remote_copy(
            src_ref=src, dst_ref=dst, send_sem=send, recv_sem=recv, device_id=(dp, seq), device_id_type=MESH
        )

    def send(ref, group, recv, dp):
        remote(ref, ref, send_sem.at[group], recv, dp, me).start()

    def arrived(ref, sem):
        remote(ref, ref, send_sem.at[0], sem, sibling, me).wait_recv()

    def exchange(source, landing, group, recv):
        each_other(lambda seq: remote(source.at[seq], landing.at[me], send_sem.at[group], recv, me_dp, seq).start())

    W_LEFT0, W_LEFT1, W_RIGHT0, W_RIGHT1, W_OPP0, W_OPP1, W_SIB, W_SIB_LEFT, W_SIB_RIGHT, W_SIB_OPP = range(10)
    low, high = pl.ds(0, half), pl.ds(half, half)
    send(wall.at[me_dp, low], 0, w_sem.at[W_LEFT0], right)
    send(wall.at[me_dp, high], 0, w_sem.at[W_RIGHT1], left)
    exchange(a_send, a_recv, 1, a_sem)
    send(wall.at[me_dp, high], 0, w_sem.at[W_LEFT1], right)
    send(wall.at[me_dp, low], 0, w_sem.at[W_RIGHT0], left)
    send(wall.at[me_dp], 0, w_sem.at[W_SIB], sibling)

    loads[3].wait()
    causal = lax.broadcasted_iota(jnp.int32, (block, block), 0) >= lax.broadcasted_iota(
        jnp.int32, (block, block), 1
    )
    for h in range(heads):
        cols = slice(h * DH, (h + 1) * DH)
        near = jnp.where(causal, dot(q[:, cols], k[:, cols], (1, 1)), 0.0).astype(BF16)
        attend[h] = near
        part[h] = dot(near, v[:, cols], (1, 0))

    arrived(wall.at[left, low], w_sem.at[W_LEFT0])
    send(wall.at[left, low], 0, w_sem.at[W_OPP0], right)
    arrived(wall.at[right, high], w_sem.at[W_RIGHT1])
    send(wall.at[right, high], 0, w_sem.at[W_OPP1], left)

    arrived(a_recv.at[pl.ds(0, seqs - 1)], a_sem)

    def forward_sum(s, total):
        p_send[s] = total.astype(BF16)
        return total + a_recv[s].astype(F32)

    lax.fori_loop(0, seqs, forward_sum, jnp.zeros((16, DH), F32), unroll=8)
    prior[me] = p_send[me]
    exchange(p_send, prior, 3, p_sem.at[y])

    arrived(wall.at[left, high], w_sem.at[W_LEFT1])
    send(wall.at[left], 0, w_sem.at[W_SIB_LEFT], sibling)
    arrived(wall.at[right, low], w_sem.at[W_RIGHT0])
    send(wall.at[right], 0, w_sem.at[W_SIB_RIGHT], sibling)
    arrived(wall.at[opposite, low], w_sem.at[W_OPP0])
    arrived(wall.at[opposite, high], w_sem.at[W_OPP1])
    send(wall.at[opposite], 0, w_sem.at[W_SIB_OPP], sibling)

    C_FAR, C_SIB = range(2)
    wide = 2 * DH

    def chip_cols(chip):
        return pl.ds(pl.multiple_of(chip * wide, wide), wide)

    loads[4].wait()
    for chip, dp in ((x_opposite, opposite), (x_right, right), (x_left, left)):
        remote(c.at[:, chip_cols(chip)], ccol.at[x, core], send_sem.at[2], c_sem.at[C_FAR], dp, me).start()
    ccol[x, core] = c[:, chip_cols(x)]

    arrived(wall.at[sibling], w_sem.at[W_SIB])
    arrived(wall.at[left_s], w_sem.at[W_SIB_LEFT])
    arrived(wall.at[right_s], w_sem.at[W_SIB_RIGHT])
    arrived(wall.at[opposite_s], w_sem.at[W_SIB_OPP])
    dn[...] = dot(c[...], wall[...].reshape(dps * block, heads * DH), (1, 0))

    N_LEFT0, N_LEFT1, N_RIGHT0, N_RIGHT1, N_OPP0, N_OPP1, N_SIB = range(7)
    pairs = heads // 2

    def middle(h):
        mixed = part[h] + dot(q[:, head_cols(h)], prior[pl.ds(h * 8, 8)].reshape(DH, DH), (1, 0))
        inverse = lax.rsqrt(jnp.mean(mixed * mixed, axis=-1, keepdims=True) + EPSILON)
        n = mixed * inverse
        dnormed = dn[:, head_cols(h)]
        dmix = (dnormed - n * jnp.mean(dnormed * n, axis=-1, keepdims=True)) * inverse
        dmix = dmix.astype(BF16)
        b_send[pl.ds(h * 8, 8)] = dot(q[:, head_cols(h)], dmix, (0, 0)).astype(BF16).reshape(8, 16, DH)
        dmixed[h] = dmix
        n = n.astype(BF16)
        n_send[h] = n
        normed[:, head_cols(h)] = n

    def send_states(h, own):
        for column in columns[:-1] if own else columns:
            target = h * nz + column
            remote(b_send.at[target], b_recv.at[me], send_sem.at[4], b_sem, me_dp, target).start()

    def send_normed(h):
        taker = h % 2

        def give(recv, dp):
            remote(n_send.at[h], nall.at[h // 2, me_dp], send_sem.at[5], recv, dp, me).start()

        give(n_sem.at[N_LEFT0 + core, h // 2], x_right * 2 + taker)
        give(n_sem.at[N_RIGHT0 + core, h // 2], x_left * 2 + taker)

        @pl.when(taker == other)
        def _():
            give(n_sem.at[N_SIB, 0], sibling)

    arrived(prior.at[pl.ds(0, nz - 1)], p_sem.at[y])
    near_rows = [(y + d) % ny for d in y_order[:-1][::-1]]
    group = [y] + near_rows[:3]
    for h in group[1:]:
        arrived(prior.at[pl.ds(h * 8, 8)], p_sem.at[h])
    for h in group:
        middle(h)
    b_recv[me] = b_send[me]
    for h in group[:0:-1]:
        send_states(h, False)
    send_states(y, True)
    for h in group:
        send_normed(h)
    group = near_rows[:2:-1]
    for h in group:
        arrived(prior.at[pl.ds(h * 8, 8)], p_sem.at[h])
    for h in group:
        middle(h)
    for h in group:
        send_states(h, False)
    for h in group:
        send_normed(h)

    for i in range(pairs):
        nall[i, me_dp] = n_send[2 * i + core]

    def arrived_columns(chips, sem):
        arrived(ccol.at[pl.ds(0, chips), 0], sem)

    arrived_columns(nx - 1, c_sem.at[C_FAR])
    for chip in range(nx):
        send(ccol.at[chip, core], 2, c_sem.at[C_SIB], sibling)

    for h in range(heads):
        cols = slice(h * DH, (h + 1) * DH)
        dmix = dmixed[h]
        back = jnp.where(causal, dot(dmix, v[:, cols], (1, 1)), 0.0).astype(BF16)
        grad_q = dot(back, k[:, cols], (1, 0)) + dot(dmix, prior[h * 8 : h * 8 + 8].reshape(DH, DH), (1, 1))
        gq_v[:, cols] = grad_q.astype(BF16)
        gk_part[h] = dot(back, q[:, cols], (0, 0))
        gv_part[h] = dot(attend[h], dmix, (0, 0))
    stores = [pltpu.make_async_copy(gq_v, gq_hbm, store_sem.at[0])]
    stores[0].start()

    mine = [(h // 2 + pairs) % pairs for h in [y - core + 8, y - core + 10, y - core + 6, y - core + 12]]
    for i in mine:
        arrived(nall.at[i, x_left * 2], n_sem.at[N_LEFT0, i])
        send(nall.at[i, x_left * 2], 5, n_sem.at[N_OPP0, 0], right)
        arrived(nall.at[i, x_right * 2 + 1], n_sem.at[N_RIGHT1, i])
        send(nall.at[i, x_right * 2 + 1], 5, n_sem.at[N_OPP1, 0], left)

    for d in range(dps):
        out_v[:, d * DH : (d + 1) * DH] = dot(normed[...], wall[d], (1, 1)).astype(BF16)
    stores.append(pltpu.make_async_copy(out_v, out_hbm, store_sem.at[1]))
    stores[1].start()

    arrived(b_recv.at[pl.ds(0, seqs - 1)], b_sem)

    def backward_sum(i, total):
        s = seqs - 1 - i
        l_send[s] = total.astype(BF16)
        return total + b_recv[s].astype(F32)

    lax.fori_loop(0, seqs, backward_sum, jnp.zeros((16, DH), F32), unroll=8)
    later[me] = l_send[me]
    exchange(l_send, later, 6, l_sem.at[y])

    arrived_columns(nx, c_sem.at[C_SIB])
    for chip in range(nx):
        for at in range(2):
            tokens = slice((2 * chip + at) * block, (2 * chip + at + 1) * block)
            ccolt[0:DH, tokens] = ccol[chip, at, :, 0:DH].T
            ccolt[DH:wide, tokens] = ccol[chip, at, :, DH:wide].T

    def arrived_heads(sem):
        arrived(nall.at[0, pl.ds(0, pairs)], sem)

    for i in range(pairs):
        arrived(nall.at[i, x_left * 2 + 1], n_sem.at[N_LEFT1, i])
        arrived(nall.at[i, x_right * 2], n_sem.at[N_RIGHT0, i])
    arrived_heads(n_sem.at[N_SIB, 0])
    arrived_heads(n_sem.at[N_OPP0, 0])
    arrived_heads(n_sem.at[N_OPP1, 0])

    factor = 1.0 / math.sqrt(dps * block * seqs)
    for i in range(pairs):
        g_tile[i] = dot(ccolt[...], nall[i].reshape(dps * block, DH), (1, 0)) * factor
        for at in range(2):
            for r in range(2):
                rows = g_tile[i, pl.ds(at * DH + r, seqs, stride=2), :]
                g_rows[pl.ds(4 * i + 2 * at + r, seqs, stride=16), :] = rows

    for s in range(seqs):
        g_send[s] = g_rows[s * 16 : s * 16 + 16, :].astype(BF16)
    g_recv[me] = g_send[me]
    exchange(g_send, g_recv, 7, g_sem)

    arrived(later.at[pl.ds(0, nz - 1)], l_sem.at[y])
    for h in near_rows:
        arrived(later.at[pl.ds(h * 8, 8)], l_sem.at[h])
    for h in range(heads):
        cols = slice(h * DH, (h + 1) * DH)
        state = later[h * 8 : h * 8 + 8].reshape(DH, DH)
        gk_v[:, cols] = (gk_part[h] + dot(v[:, cols], state, (1, 1))).astype(BF16)
        gv_v[:, cols] = (gv_part[h] + dot(k[:, cols], state, (1, 0))).astype(BF16)
    stores.append(pltpu.make_async_copy(gk_v, gk_hbm, store_sem.at[2]))
    stores.append(pltpu.make_async_copy(gv_v, gv_hbm, store_sem.at[3]))
    stores[2].start()
    stores[3].start()

    def sent(ref, i):
        remote(ref, ref, send_sem.at[i], a_sem, sibling, me).wait_send()

    sent(wall.at[pl.ds(0, 7)], 0)
    sent(a_send.at[pl.ds(0, seqs - 1)], 1)
    sent(ccol.at[pl.ds(0, nx - 1), 0], 2)
    sent(ccol.at[pl.ds(0, nx), 0], 2)
    sent(p_send.at[pl.ds(0, seqs - 1)], 3)
    sent(b_send.at[pl.ds(0, seqs - 1)], 4)
    sent(nall.at[pl.ds(0, 3)], 5)
    sent(nall.at[0, pl.ds(0, 4)], 5)
    sent(l_send.at[pl.ds(0, seqs - 1)], 6)

    arrived(g_recv.at[pl.ds(0, seqs - 1)], g_sem)
    total = lax.fori_loop(0, seqs, lambda s, t: t + g_recv[s].astype(F32), jnp.zeros((16, DH), F32), unroll=8)
    g_sum[...] = total
    swap = remote(g_sum, g_other, send_sem.at[8], swap_sem, sibling, me)
    swap.start()
    swap.wait()
    theirs = g_other[...]
    even = jnp.where(core == 0, total, theirs)
    odd = jnp.where(core == 0, theirs, total)
    for h in range(heads):
        source = even if h % 2 == 0 else odd
        at = 4 * (h // 2)
        gw_v[:, h * DH : (h + 1) * DH] = jnp.where(core == 0, source[at : at + 2], source[at + 2 : at + 4])
    stores.append(pltpu.make_async_copy(gw_v, gw_hbm, store_sem.at[4]))
    stores[4].start()
    sent(g_send.at[pl.ds(0, seqs - 1)], 7)
    for store in stores:
        store.wait()


def place(*refs):
    count = len(refs) // 2
    sems = refs[-1]
    copies = [pltpu.make_async_copy(refs[i], refs[count + i], sems.at[i]) for i in range(count)]
    for copy in copies:
        copy.start()
    for copy in copies:
        copy.wait()


def local(sizes, queries, keys, values, cotangent, out_weight):
    dps, ny, nz, heads = sizes
    _, block, features = queries.shape
    seqs = ny * nz
    shapes = [jax.ShapeDtypeStruct((block, features), BF16)] * 4 + [jax.ShapeDtypeStruct((2, features), F32)]
    arguments = (queries[0], keys[0], values[0], cotangent[0], out_weight)
    states = pltpu.VMEM((seqs, 16, DH), BF16)
    whole = pltpu.VMEM((block, features), BF16)
    per_head = pltpu.VMEM((heads, block, DH), F32)
    dma = pltpu.SemaphoreType.DMA
    piece = pltpu.VMEM((16, DH), F32)
    out = pl.pallas_call(
        functools.partial(kernel, sizes),
        out_shape=shapes,
        in_specs=[pl.BlockSpec(memory_space=pl.ANY)] * 5,
        out_specs=[pl.BlockSpec(memory_space=pl.ANY)] * 5,
        scratch_shapes=[
            whole, whole, whole, whole,
            pltpu.VMEM((dps, block, features), BF16),
            pltpu.VMEM((block, features), F32),
            states, states, states, states,
            states, states, states, states,
            pltpu.VMEM((heads, block, block), BF16),
            per_head,
            whole,
            pltpu.VMEM((heads, block, DH), BF16),
            pltpu.VMEM((heads, block, DH), BF16),
            pltpu.VMEM((heads // 2, dps, block, DH), BF16),
            pltpu.VMEM((dps // 2, 2, block, 2 * DH), BF16),
            pltpu.VMEM((2 * DH, dps * block), BF16),
            per_head, per_head,
            pltpu.VMEM((heads // 2, 2 * DH, DH), F32),
            pltpu.VMEM((seqs * 16, DH), F32),
            states, states, piece, piece,
            whole, whole, whole, whole,
            pltpu.VMEM((2, features), F32),
            dma((5,)), dma((5,)), dma((9,)), dma, dma((heads,)), dma, dma((heads,)), dma,
            dma((10,)), dma((2,)), dma((7, heads // 2)), dma,
        ],
        compiler_params=pltpu.CompilerParams(
            collective_id=0, has_side_effects=True, vmem_limit_bytes=VMEM_LIMIT
        ),
        name="layer",
    )(*(pltpu.with_memory_space_constraint(a, pltpu.HBM) for a in arguments))
    out = pl.pallas_call(
        place,
        out_shape=shapes,
        in_specs=[pl.BlockSpec(memory_space=pl.ANY)] * 5,
        out_specs=[pl.BlockSpec(memory_space=pl.ANY)] * 5,
        scratch_shapes=[dma((5,))],
        compiler_params=pltpu.CompilerParams(vmem_limit_bytes=VMEM_LIMIT),
        name="place",
    )(*out)
    return tuple(part[None] for part in out[:4]) + (out[4],)


def solution(mesh):
    seqs = mesh.shape["seq"]
    ny = nz = math.isqrt(seqs)
    sizes = (mesh.shape["dp"], ny, nz, 8)
    tokens = P("dp", "seq", None)
    return jax.shard_map(
        functools.partial(local, sizes),
        mesh=mesh,
        in_specs=(tokens, tokens, tokens, tokens, P("dp", None)),
        out_specs=(tokens, tokens, tokens, tokens, P(("dp", "seq"), None)),
        check_vma=False,
    )
```

time: 82.5 us -> 63.9 us (0.77)
  Pallas kernels: 73.4 us -> 63.1 us
  local copies, waits for them, and re-layouts: 8.15 us -> 0 us
    pallas_call x1 -> x2, Pallas kernels: 73.4 us -> 63.1 us  [the longest x1 62.1 us: local(): pl.pallas_call(functools.partial(kernel, sizes), out_shape=shapes, in_spe...]
    unnamed x15 -> x0, local copies, waits for them, and re-layouts: 8.15 us -> none
where the time goes in v2:
time: 63.9 us; the launch traced here: 63.7 us
  Pallas kernels  63.1 us (99%)
  between operations  0.64 us (1%)
    pallas_call x1, Pallas kernels, local(): pl.pallas_call(functools.partial(kernel, sizes), out_shape=shapes, in_spe...  62.1 us

profile of v2, /device:TPU:1, one launch (start us, length us, event | category | flops | bytes accessed | tf_op | source)
XLA Modules:
  0.0 63.7 jit_solution(10622341550909410144)
XLA Ops:
  0.6 62.1 %layer.1 = (bf16[128,1024]{1,0:T(8,128)(2,1)S(1)}, bf16[128,1024]{1,0:T(8,128)(2,1)S(1)}, bf16[128,1024]{1,0:T(8,128)(2,1)S(1)}, bf16[128,1024]{1,0:T(8,128)(2,1)S(1)}, f32[2,1024]{1,0:T(2,128)S(1)}) custom-call(bf16[128,1024]{1,0:T(8,128)(2,1)} %bitcast.8, bf16[128,1024]{1,0:T(8,128)(2,1)} %bitcast.9, bf16[128,1024]{1,0:T(8,128)(2,1)} %bitcast.10, ...), custom_call_target="tpu_custom_call" | custom-call | tf_op jit(solution)/shard_map/layer/pallas_call | solution.py:375
  62.7 1.0 %place.1 = (bf16[128,1024]{1,0:T(8,128)(2,1)}, bf16[128,1024]{1,0:T(8,128)(2,1)}, bf16[128,1024]{1,0:T(8,128)(2,1)}, bf16[128,1024]{1,0:T(8,128)(2,1)}, f32[2,1024]{1,0:T(2,128)}) custom-call(bf16[128,1024]{1,0:T(8,128)(2,1)S(1)} %get-tuple-element.15.refs_0_, bf16[128,1024]{1,0:T(8,128)(2,1)S(1)} %get-tuple-element.16.refs_1_, ...), custom_call_target="tpu_custom_call" | custom-call | tf_op jit(solution)/shard_map/place/pallas_call | solution.py:408

commit v3 on v2

v3 whole, which is shorter than its diff:
```python
import functools
import math

import jax
import jax.numpy as jnp
from jax import lax
from jax.experimental import pallas as pl
from jax.experimental.pallas import tpu as pltpu
from jax.sharding import PartitionSpec as P

MESH = pl.DeviceIdType.MESH
DH = 128
EPSILON = 1e-05
BF16 = jnp.bfloat16
F32 = jnp.float32
VMEM_LIMIT = 40 * 1024 * 1024


def dot(left, right, contract):
    return lax.dot_general(left, right, ((contract[:1], contract[1:]), ((), ())), preferred_element_type=F32)


def head_cols(h):
    return pl.ds(pl.multiple_of(h * DH, DH), DH)


def apart(offset, count):
    return min(offset, count - offset)


def far_first(ny, nz):
    offsets = [(dy, dz) for dy in range(ny) for dz in range(nz)]
    return sorted(offsets, key=lambda o: -(apart(o[0], ny) + apart(o[1], nz)))


def kernel(
    sizes,
    q_hbm, k_hbm, v_hbm, c_hbm, w_hbm,
    out_hbm, gq_hbm, gk_hbm, gv_hbm, gw_hbm,
    q, k, v, c, wall, dn,
    a_send, a_recv, p_send, prior,
    b_send, b_recv, l_send, later,
    attend, part, normed, dmixed, n_send, nall, ccolt,
    gk_part, gv_part, g_tile, g_rows, g_send, g_recv, g_out, g_in,
    out_v, gq_v, gk_v, gv_v, gw_v,
    load_sem, store_sem, send_sem, a_sem, p_sem, b_sem, l_sem, g_sem,
    w_sem, c_sem, n_sem, swap_sem,
):
    dps, ny, nz, heads = sizes
    nx = dps // 2
    seqs = ny * nz
    block = q.shape[0]
    half = block // 2
    me_dp, me = lax.axis_index("dp"), lax.axis_index("seq")
    x, core = me_dp // 2, me_dp % 2
    y, z = me // nz, me % nz
    x_right, x_left, x_opposite = (x + 1) % nx, (x + nx - 1) % nx, (x + 2) % nx
    other = 1 - core
    right, left, opposite = x_right * 2 + core, x_left * 2 + core, x_opposite * 2 + core
    sibling = x * 2 + other
    right_s, left_s, opposite_s = x_right * 2 + other, x_left * 2 + other, x_opposite * 2 + other

    rows = [(y + d) % ny for d in range(ny)]
    columns = [(z + d) % nz for d in range(nz)]
    others = far_first(ny, nz)[:-1]
    mine = z * ny + y
    near_columns = sorted(range(nz), key=lambda d: apart(d, nz))
    halves = (near_columns[: nz // 2], near_columns[nz // 2 :])

    loads = [
        pltpu.make_async_copy(src, dst, load_sem.at[i])
        for i, (src, dst) in enumerate(
            [(k_hbm, k), (v_hbm, v), (w_hbm, wall.at[me_dp]), (q_hbm, q), (c_hbm, c)]
        )
    ]
    for load in loads:
        load.start()

    barrier = pltpu.get_barrier_semaphore()

    def greet(dp, seq):
        pl.semaphore_signal(barrier, inc=1, device_id=(dp, seq), device_id_type=MESH)

    for dy, dz in others:
        greet(me_dp, rows[dy] * nz + columns[dz])
    for dp in (opposite, opposite_s, right, left, right_s, left_s, sibling):
        greet(dp, me)

    loads[0].wait()
    loads[1].wait()
    for h in range(heads):
        cols = slice(h * DH, (h + 1) * DH)
        a_send[h * 8 : h * 8 + 8] = dot(k[:, cols], v[:, cols], (0, 0)).astype(BF16).reshape(8, 16, DH)
    a_recv[me] = a_send[mine]
    loads[2].wait()
    pl.semaphore_wait(barrier, seqs - 1 + dps - 1)

    def remote(src, dst, send, recv, dp, seq):
        return pltpu.make_async_remote_copy(
            src_ref=src, dst_ref=dst, send_sem=send, recv_sem=recv, device_id=(dp, seq), device_id_type=MESH
        )

    def send(ref, group, recv, dp):
        remote(ref, ref, send_sem.at[group], recv, dp, me).start()

    def arrived(ref, sem):
        remote(ref, ref, send_sem.at[0], sem, sibling, me).wait_recv()

    def to_owners(source, landing, group, recv, offsets):
        for dy, dz in offsets:
            row, column = rows[dy], columns[dz]
            piece = source.at[column * ny + row]
            remote(piece, landing.at[me], send_sem.at[group], recv, me_dp, row * nz + column).start()

    def give_back(source, landing, slot, group, recv):
        for dy, dz in others:
            seq = rows[dy] * nz + columns[dz]
            remote(source.at[seq], landing.at[slot], send_sem.at[group], recv, me_dp, seq).start()

    def given_back(landing, dz, recv):
        count = ny - 1 if dz == 0 else ny
        arrived(landing.at[pl.ds(0, count)], recv.at[columns[dz]])

    W_LEFT0, W_LEFT1, W_RIGHT0, W_RIGHT1, W_OPP0, W_OPP1, W_SIB, W_SIB_LEFT, W_SIB_RIGHT, W_SIB_OPP = range(10)
    low, high = pl.ds(0, half), pl.ds(half, half)
    send(wall.at[me_dp, low], 0, w_sem.at[W_LEFT0], right)
    send(wall.at[me_dp, high], 0, w_sem.at[W_RIGHT1], left)
    to_owners(a_send, a_recv, 1, a_sem, others)
    send(wall.at[me_dp, high], 0, w_sem.at[W_LEFT1], right)
    send(wall.at[me_dp, low], 0, w_sem.at[W_RIGHT0], left)
    send(wall.at[me_dp], 0, w_sem.at[W_SIB], sibling)

    loads[3].wait()
    causal = lax.broadcasted_iota(jnp.int32, (block, block), 0) >= lax.broadcasted_iota(
        jnp.int32, (block, block), 1
    )
    for h in range(heads):
        cols = slice(h * DH, (h + 1) * DH)
        near = jnp.where(causal, dot(q[:, cols], k[:, cols], (1, 1)), 0.0).astype(BF16)
        attend[h] = near
        part[h] = dot(near, v[:, cols], (1, 0))

    arrived(wall.at[left, low], w_sem.at[W_LEFT0])
    send(wall.at[left, low], 0, w_sem.at[W_OPP0], right)
    arrived(wall.at[right, high], w_sem.at[W_RIGHT1])
    send(wall.at[right, high], 0, w_sem.at[W_OPP1], left)

    loads[4].wait()
    own_c = ccolt.at[:, head_cols(me_dp)]
    for h in range(heads):
        rows_h = slice(h * DH, (h + 1) * DH)
        ccolt[rows_h, head_cols(me_dp)] = c[:, rows_h].T
    C_LEFT, C_RIGHT, C_OPP, C_SIB, C_SIB_LEFT, C_SIB_RIGHT, C_SIB_OPP = range(7)
    send(own_c, 2, c_sem.at[C_LEFT], right)
    send(own_c, 2, c_sem.at[C_RIGHT], left)
    send(own_c, 2, c_sem.at[C_OPP], opposite)
    send(own_c, 2, c_sem.at[C_SIB], sibling)

    arrived(a_recv.at[pl.ds(0, seqs - 1)], a_sem)

    def forward_sum(s, total):
        p_send[s] = total.astype(BF16)
        return total + a_recv[s].astype(F32)

    lax.fori_loop(0, seqs, forward_sum, jnp.zeros((16, DH), F32), unroll=8)
    prior[mine] = p_send[me]
    give_back(p_send, prior, mine, 3, p_sem.at[z])

    arrived(wall.at[left, high], w_sem.at[W_LEFT1])
    send(wall.at[left], 0, w_sem.at[W_SIB_LEFT], sibling)
    arrived(wall.at[right, low], w_sem.at[W_RIGHT0])
    send(wall.at[right], 0, w_sem.at[W_SIB_RIGHT], sibling)
    arrived(wall.at[opposite, low], w_sem.at[W_OPP0])
    arrived(wall.at[opposite, high], w_sem.at[W_OPP1])
    send(wall.at[opposite], 0, w_sem.at[W_SIB_OPP], sibling)

    arrived(wall.at[sibling], w_sem.at[W_SIB])
    arrived(wall.at[left_s], w_sem.at[W_SIB_LEFT])
    arrived(wall.at[right_s], w_sem.at[W_SIB_RIGHT])
    arrived(wall.at[opposite_s], w_sem.at[W_SIB_OPP])
    dn[...] = dot(c[...], wall[...].reshape(dps * block, heads * DH), (1, 0))

    for half_dz in halves:
        group = [columns[dz] for dz in half_dz]
        for dz in half_dz:
            given_back(prior, dz, p_sem)
        kept = []
        for h in group:
            mixed = part[h] + dot(q[:, head_cols(h)], prior[pl.ds(h * 8, 8)].reshape(DH, DH), (1, 0))
            inverse = lax.rsqrt(jnp.mean(mixed * mixed, axis=-1, keepdims=True) + EPSILON)
            n = mixed * inverse
            n_send[h] = n.astype(BF16)
            kept.append((n, inverse))
        for h in group:
            @pl.when(h != me_dp)
            def _(h=h):
                remote(n_send.at[h], nall.at[me_dp], send_sem.at[5], n_sem, h, me).start()

        for h, (n, inverse) in zip(group, kept):
            dnormed = dn[:, head_cols(h)]
            dmix = (dnormed - n * jnp.mean(dnormed * n, axis=-1, keepdims=True)) * inverse
            dmix = dmix.astype(BF16)
            u = dot(q[:, head_cols(h)], dmix, (0, 0))
            b_send[pl.ds(h * 8, 8)] = u.astype(BF16).reshape(8, 16, DH)
            dmixed[h] = dmix
            normed[:, head_cols(h)] = n.astype(BF16)
        to_owners(b_send, b_recv, 4, b_sem, [o for o in others if o[1] in half_dz])
    b_recv[me] = b_send[mine]
    nall[me_dp] = n_send[me_dp]

    for dp, here, there in ((left, C_LEFT, C_SIB_LEFT), (right, C_RIGHT, C_SIB_RIGHT), (opposite, C_OPP, C_SIB_OPP)):
        tokens = ccolt.at[:, head_cols(dp)]
        arrived(tokens, c_sem.at[here])
        send(tokens, 2, c_sem.at[there], sibling)

    for dp, there in ((sibling, C_SIB), (left_s, C_SIB_LEFT), (right_s, C_SIB_RIGHT), (opposite_s, C_SIB_OPP)):
        arrived(ccolt.at[:, head_cols(dp)], c_sem.at[there])
    arrived(nall.at[pl.ds(0, dps - 1)], n_sem)
    factor = 1.0 / math.sqrt(dps * block * seqs)
    g_tile[...] = dot(ccolt[...], nall[...].reshape(dps * block, DH), (1, 0)) * factor
    for d in range(dps):
        for r in range(2):
            g_rows[pl.ds(2 * d + r, seqs, stride=16), :] = g_tile[pl.ds(d * block + r, seqs, stride=2), :]
    for s in range(seqs):
        g_send[s] = g_rows[s * 16 : s * 16 + 16, :].astype(BF16)
    g_recv[me] = g_send[me]

    def sum_back():
        arrived(b_recv.at[pl.ds(0, seqs - 1)], b_sem)

        def backward_sum(i, total):
            s = seqs - 1 - i
            l_send[s] = total.astype(BF16)
            return total + b_recv[s].astype(F32)

        lax.fori_loop(0, seqs, backward_sum, jnp.zeros((16, DH), F32), unroll=8)
        later[mine] = l_send[me]
        give_back(l_send, later, mine, 6, l_sem.at[z])

    give_back(g_send, g_recv, me, 7, g_sem)
    sum_back()

    for h in range(heads):
        cols = slice(h * DH, (h + 1) * DH)
        dmix = dmixed[h]
        back = jnp.where(causal, dot(dmix, v[:, cols], (1, 1)), 0.0).astype(BF16)
        grad_q = dot(back, k[:, cols], (1, 0)) + dot(dmix, prior[h * 8 : h * 8 + 8].reshape(DH, DH), (1, 1))
        gq_v[:, cols] = grad_q.astype(BF16)
        gk_part[h] = dot(back, q[:, cols], (0, 0))
        gv_part[h] = dot(attend[h], dmix, (0, 0))
    stores = [pltpu.make_async_copy(gq_v, gq_hbm, store_sem.at[0])]
    stores[0].start()

    for d in range(dps):
        out_v[:, d * DH : (d + 1) * DH] = dot(normed[...], wall[d], (1, 1)).astype(BF16)
    stores.append(pltpu.make_async_copy(out_v, out_hbm, store_sem.at[1]))
    stores[1].start()

    arrived(g_recv.at[pl.ds(0, seqs - 1)], g_sem)
    total = lax.fori_loop(0, seqs, lambda s, t: t + g_recv[s].astype(F32), jnp.zeros((16, DH), F32), unroll=8)
    for d in range(dps):
        g_out[d] = total[2 * d : 2 * d + 2]
    g_in[me_dp] = g_out[me_dp]
    for dp in (opposite, opposite_s, right, right_s, left, left_s, sibling):
        remote(g_out.at[dp], g_in.at[me_dp], send_sem.at[8], swap_sem, dp, me).start()

    for half_dz in halves:
        for dz in half_dz:
            given_back(later, dz, l_sem)
        for dz in half_dz:
            h = columns[dz]
            cols = head_cols(h)
            state = later[pl.ds(h * 8, 8)].reshape(DH, DH)
            gk_v[:, cols] = (gk_part[h] + dot(v[:, cols], state, (1, 1))).astype(BF16)
            gv_v[:, cols] = (gv_part[h] + dot(k[:, cols], state, (1, 0))).astype(BF16)
    stores.append(pltpu.make_async_copy(gk_v, gk_hbm, store_sem.at[2]))
    stores.append(pltpu.make_async_copy(gv_v, gv_hbm, store_sem.at[3]))
    stores[2].start()
    stores[3].start()

    def sent(ref, i):
        remote(ref, ref, send_sem.at[i], a_sem, sibling, me).wait_send()

    sent(wall.at[pl.ds(0, 7)], 0)
    sent(a_send.at[pl.ds(0, seqs - 1)], 1)
    sent(ccolt.at[:, pl.ds(0, 7 * block)], 2)
    sent(p_send.at[pl.ds(0, seqs - 1)], 3)
    sent(b_send.at[pl.ds(0, seqs - 1)], 4)
    sent(nall.at[pl.ds(0, dps - 1)], 5)
    sent(l_send.at[pl.ds(0, seqs - 1)], 6)

    sent(g_send.at[pl.ds(0, seqs - 1)], 7)
    sent(g_out.at[pl.ds(0, dps - 1)], 8)
    arrived(g_in.at[pl.ds(0, dps - 1)], swap_sem)
    for d in range(dps):
        gw_v[:, d * DH : (d + 1) * DH] = g_in[d]
    stores.append(pltpu.make_async_copy(gw_v, gw_hbm, store_sem.at[4]))
    stores[4].start()
    for store in stores:
        store.wait()


def place(*refs):
    count = len(refs) // 2
    sems = refs[-1]
    copies = [pltpu.make_async_copy(refs[i], refs[count + i], sems.at[i]) for i in range(count)]
    for copy in copies:
        copy.start()
    for copy in copies:
        copy.wait()


def local(sizes, queries, keys, values, cotangent, out_weight):
    dps, ny, nz, heads = sizes
    _, block, features = queries.shape
    seqs = ny * nz
    shapes = [jax.ShapeDtypeStruct((block, features), BF16)] * 4 + [jax.ShapeDtypeStruct((2, features), F32)]
    arguments = (queries[0], keys[0], values[0], cotangent[0], out_weight)
    states = pltpu.VMEM((seqs, 16, DH), BF16)
    whole = pltpu.VMEM((block, features), BF16)
    per_head = pltpu.VMEM((heads, block, DH), F32)
    dma = pltpu.SemaphoreType.DMA
    piece = pltpu.VMEM((dps, 2, DH), F32)
    out = pl.pallas_call(
        functools.partial(kernel, sizes),
        out_shape=shapes,
        in_specs=[pl.BlockSpec(memory_space=pl.ANY)] * 5,
        out_specs=[pl.BlockSpec(memory_space=pl.ANY)] * 5,
        scratch_shapes=[
            whole, whole, whole, whole,
            pltpu.VMEM((dps, block, features), BF16),
            pltpu.VMEM((block, features), F32),
            states, states, states, states,
            states, states, states, states,
            pltpu.VMEM((heads, block, block), BF16),
            per_head,
            whole,
            pltpu.VMEM((heads, block, DH), BF16),
            pltpu.VMEM((heads, block, DH), BF16),
            pltpu.VMEM((dps, block, DH), BF16),
            pltpu.VMEM((features, dps * block), BF16),
            per_head, per_head,
            pltpu.VMEM((features, DH), F32),
            pltpu.VMEM((seqs * 16, DH), F32),
            states, states, piece, piece,
            whole, whole, whole, whole,
            pltpu.VMEM((2, features), F32),
            dma((5,)), dma((5,)), dma((9,)), dma, dma((heads,)), dma, dma((heads,)), dma,
            dma((10,)), dma((7,)), dma, dma,
        ],
        compiler_params=pltpu.CompilerParams(
            collective_id=0, has_side_effects=True, vmem_limit_bytes=VMEM_LIMIT
        ),
        name="layer",
    )(*(pltpu.with_memory_space_constraint(a, pltpu.HBM) for a in arguments))
    out = pl.pallas_call(
        place,
        out_shape=shapes,
        in_specs=[pl.BlockSpec(memory_space=pl.ANY)] * 5,
        out_specs=[pl.BlockSpec(memory_space=pl.ANY)] * 5,
        scratch_shapes=[dma((5,))],
        compiler_params=pltpu.CompilerParams(vmem_limit_bytes=VMEM_LIMIT),
        name="place",
    )(*out)
    return tuple(part[None] for part in out[:4]) + (out[4],)


def solution(mesh):
    seqs = mesh.shape["seq"]
    ny = nz = math.isqrt(seqs)
    sizes = (mesh.shape["dp"], ny, nz, 8)
    tokens = P("dp", "seq", None)
    return jax.shard_map(
        functools.partial(local, sizes),
        mesh=mesh,
        in_specs=(tokens, tokens, tokens, tokens, P("dp", None)),
        out_specs=(tokens, tokens, tokens, tokens, P(("dp", "seq"), None)),
        check_vma=False,
    )
```

time: 63.9 us -> 60 us (0.939)
  Pallas kernels: 63.1 us -> 59.2 us
    pallas_call x1, Pallas kernels: 62.1 us -> 58.2 us  [local(): pl.pallas_call(functools.partial(kernel, sizes), out_shape=shapes, in_spe...]
where the time goes in v3:
time: 60 us; the launch traced here: 59.8 us
  Pallas kernels  59.2 us (99%)
  between operations  0.64 us (1%)
    pallas_call x1, Pallas kernels, local(): pl.pallas_call(functools.partial(kernel, sizes), out_shape=shapes, in_spe...  58.2 us

profile of v3, /device:TPU:1, one launch (start us, length us, event | category | flops | bytes accessed | tf_op | source)
XLA Modules:
  0.0 59.8 jit_solution(10996731701136128024)
XLA Ops:
  0.6 58.2 %layer.1 = (bf16[128,1024]{1,0:T(8,128)(2,1)S(1)}, bf16[128,1024]{1,0:T(8,128)(2,1)S(1)}, bf16[128,1024]{1,0:T(8,128)(2,1)S(1)}, bf16[128,1024]{1,0:T(8,128)(2,1)S(1)}, f32[2,1024]{1,0:T(2,128)S(1)}) custom-call(bf16[128,1024]{1,0:T(8,128)(2,1)} %bitcast.8, bf16[128,1024]{1,0:T(8,128)(2,1)} %bitcast.9, bf16[128,1024]{1,0:T(8,128)(2,1)} %bitcast.10, ...), custom_call_target="tpu_custom_call" | custom-call | tf_op jit(solution)/shard_map/layer/pallas_call | solution.py:324
  58.8 1.0 %place.1 = (bf16[128,1024]{1,0:T(8,128)(2,1)}, bf16[128,1024]{1,0:T(8,128)(2,1)}, bf16[128,1024]{1,0:T(8,128)(2,1)}, bf16[128,1024]{1,0:T(8,128)(2,1)}, f32[2,1024]{1,0:T(2,128)}) custom-call(bf16[128,1024]{1,0:T(8,128)(2,1)S(1)} %get-tuple-element.15.refs_0_, bf16[128,1024]{1,0:T(8,128)(2,1)S(1)} %get-tuple-element.16.refs_1_, ...), custom_call_target="tpu_custom_call" | custom-call | tf_op jit(solution)/shard_map/place/pallas_call | solution.py:356

commit v4 on v3

--- a/solution.py
+++ b/solution.py
@@ -36,14 +36,13 @@
 def kernel(
     sizes,
     q_hbm, k_hbm, v_hbm, c_hbm, w_hbm,
-    out_hbm, gq_hbm, gk_hbm, gv_hbm, gw_hbm,
+    out_v, gq_v, gk_v, gv_v, gw_v,
     q, k, v, c, wall, dn,
     a_send, a_recv, p_send, prior,
     b_send, b_recv, l_send, later,
     attend, part, normed, dmixed, n_send, nall, ccolt,
     gk_part, gv_part, g_tile, g_rows, g_send, g_recv, g_out, g_in,
-    out_v, gq_v, gk_v, gv_v, gw_v,
-    load_sem, store_sem, send_sem, a_sem, p_sem, b_sem, l_sem, g_sem,
+    load_sem, send_sem, a_sem, p_sem, b_sem, l_sem, g_sem,
     w_sem, c_sem, n_sem, swap_sem,
 ):
     dps, ny, nz, heads = sizes
@@ -149,7 +148,10 @@
     own_c = ccolt.at[:, head_cols(me_dp)]
     for h in range(heads):
         rows_h = slice(h * DH, (h + 1) * DH)
-        ccolt[rows_h, head_cols(me_dp)] = c[:, rows_h].T
+        g_tile[rows_h, :] = c[:, rows_h].astype(F32).T
+        for r in range(2):
+            g_rows[pl.ds(2 * h + r, seqs, stride=16), :] = g_tile[pl.ds(h * DH + r, seqs, stride=2), :]
+    ccolt[:, head_cols(me_dp)] = g_rows[...].astype(BF16)
     C_LEFT, C_RIGHT, C_OPP, C_SIB, C_SIB_LEFT, C_SIB_RIGHT, C_SIB_OPP = range(7)
     send(own_c, 2, c_sem.at[C_LEFT], right)
     send(own_c, 2, c_sem.at[C_RIGHT], left)
@@ -191,11 +193,6 @@
             n = mixed * inverse
             n_send[h] = n.astype(BF16)
             kept.append((n, inverse))
-        for h in group:
-            @pl.when(h != me_dp)
-            def _(h=h):
-                remote(n_send.at[h], nall.at[me_dp], send_sem.at[5], n_sem, h, me).start()
-
         for h, (n, inverse) in zip(group, kept):
             dnormed = dn[:, head_cols(h)]
             dmix = (dnormed - n * jnp.mean(dnormed * n, axis=-1, keepdims=True)) * inverse
@@ -205,6 +202,11 @@
             dmixed[h] = dmix
             normed[:, head_cols(h)] = n.astype(BF16)
         to_owners(b_send, b_recv, 4, b_sem, [o for o in others if o[1] in half_dz])
+        for h in group:
+            @pl.when(h != me_dp)
+            def _(h=h):
+                remote(n_send.at[h], nall.at[me_dp], send_sem.at[5], n_sem, h, me).start()
+
     b_recv[me] = b_send[mine]
     nall[me_dp] = n_send[me_dp]
 
@@ -217,12 +219,8 @@
         arrived(ccolt.at[:, head_cols(dp)], c_sem.at[there])
     arrived(nall.at[pl.ds(0, dps - 1)], n_sem)
     factor = 1.0 / math.sqrt(dps * block * seqs)
-    g_tile[...] = dot(ccolt[...], nall[...].reshape(dps * block, DH), (1, 0)) * factor
-    for d in range(dps):
-        for r in range(2):
-            g_rows[pl.ds(2 * d + r, seqs, stride=16), :] = g_tile[pl.ds(d * block + r, seqs, stride=2), :]
-    for s in range(seqs):
-        g_send[s] = g_rows[s * 16 : s * 16 + 16, :].astype(BF16)
+    g = dot(ccolt[...], nall[...].reshape(dps * block, DH), (1, 0)) * factor
+    g_send[...] = g.astype(BF16).reshape(seqs, 16, DH)
     g_recv[me] = g_send[me]
 
     def sum_back():
@@ -248,13 +246,9 @@
         gq_v[:, cols] = grad_q.astype(BF16)
         gk_part[h] = dot(back, q[:, cols], (0, 0))
         gv_part[h] = dot(attend[h], dmix, (0, 0))
-    stores = [pltpu.make_async_copy(gq_v, gq_hbm, store_sem.at[0])]
-    stores[0].start()
 
     for d in range(dps):
         out_v[:, d * DH : (d + 1) * DH] = dot(normed[...], wall[d], (1, 1)).astype(BF16)
-    stores.append(pltpu.make_async_copy(out_v, out_hbm, store_sem.at[1]))
-    stores[1].start()
 
     arrived(g_recv.at[pl.ds(0, seqs - 1)], g_sem)
     total = lax.fori_loop(0, seqs, lambda s, t: t + g_recv[s].astype(F32), jnp.zeros((16, DH), F32), unroll=8)
@@ -273,10 +267,6 @@
             state = later[pl.ds(h * 8, 8)].reshape(DH, DH)
             gk_v[:, cols] = (gk_part[h] + dot(v[:, cols], state, (1, 1))).astype(BF16)
             gv_v[:, cols] = (gv_part[h] + dot(k[:, cols], state, (1, 0))).astype(BF16)
-    stores.append(pltpu.make_async_copy(gk_v, gk_hbm, store_sem.at[2]))
-    stores.append(pltpu.make_async_copy(gv_v, gv_hbm, store_sem.at[3]))
-    stores[2].start()
-    stores[3].start()
 
     def sent(ref, i):
         remote(ref, ref, send_sem.at[i], a_sem, sibling, me).wait_send()
@@ -294,10 +284,6 @@
     arrived(g_in.at[pl.ds(0, dps - 1)], swap_sem)
     for d in range(dps):
         gw_v[:, d * DH : (d + 1) * DH] = g_in[d]
-    stores.append(pltpu.make_async_copy(gw_v, gw_hbm, store_sem.at[4]))
-    stores[4].start()
-    for store in stores:
-        store.wait()
 
 
 def place(*refs):
@@ -323,9 +309,9 @@
     piece = pltpu.VMEM((dps, 2, DH), F32)
     out = pl.pallas_call(
         functools.partial(kernel, sizes),
-        out_shape=shapes,
+        out_shape=[pltpu.VMEM(s.shape, s.dtype) for s in shapes],
         in_specs=[pl.BlockSpec(memory_space=pl.ANY)] * 5,
-        out_specs=[pl.BlockSpec(memory_space=pl.ANY)] * 5,
+        out_specs=[pl.BlockSpec(memory_space=pltpu.VMEM)] * 5,
         scratch_shapes=[
             whole, whole, whole, whole,
             pltpu.VMEM((dps, block, features), BF16),
@@ -343,9 +329,7 @@
             pltpu.VMEM((features, DH), F32),
             pltpu.VMEM((seqs * 16, DH), F32),
             states, states, piece, piece,
-            whole, whole, whole, whole,
-            pltpu.VMEM((2, features), F32),
-            dma((5,)), dma((5,)), dma((9,)), dma, dma((heads,)), dma, dma((heads,)), dma,
+            dma((5,)), dma((9,)), dma, dma((heads,)), dma, dma((heads,)), dma,
             dma((10,)), dma((7,)), dma, dma,
         ],
         compiler_params=pltpu.CompilerParams(

time: 60 us -> 59.7 us (level)
  no operation moved by 1% of the time
where the time goes in v4:
time: 59.7 us; the launch traced here: 59.6 us
  Pallas kernels  59 us (99%)
  between operations  0.64 us (1%)
    pallas_call x1, Pallas kernels, local(): pl.pallas_call(functools.partial(kernel, sizes), out_shape=[pltpu.VMEM(s....  57.9 us

profile of v4, /device:TPU:1, one launch (start us, length us, event | category | flops | bytes accessed | tf_op | source)
XLA Modules:
  0.0 59.6 jit_solution(9463547147558775394)
XLA Ops:
  0.6 57.9 %layer.1 = (bf16[128,1024]{1,0:T(8,128)(2,1)S(1)}, bf16[128,1024]{1,0:T(8,128)(2,1)S(1)}, bf16[128,1024]{1,0:T(8,128)(2,1)S(1)}, bf16[128,1024]{1,0:T(8,128)(2,1)S(1)}, f32[2,1024]{1,0:T(2,128)S(1)}) custom-call(bf16[128,1024]{1,0:T(8,128)(2,1)} %bitcast.8, bf16[128,1024]{1,0:T(8,128)(2,1)} %bitcast.9, bf16[128,1024]{1,0:T(8,128)(2,1)} %bitcast.10, ...), custom_call_target="tpu_custom_call" | custom-call | tf_op jit(solution)/shard_map/layer/pallas_call | solution.py:310
  58.6 1.0 %place.1 = (bf16[128,1024]{1,0:T(8,128)(2,1)}, bf16[128,1024]{1,0:T(8,128)(2,1)}, bf16[128,1024]{1,0:T(8,128)(2,1)}, bf16[128,1024]{1,0:T(8,128)(2,1)}, f32[2,1024]{1,0:T(2,128)}) custom-call(bf16[128,1024]{1,0:T(8,128)(2,1)S(1)} %get-tuple-element.15.refs_0_, bf16[128,1024]{1,0:T(8,128)(2,1)S(1)} %get-tuple-element.16.refs_1_, ...), custom_call_target="tpu_custom_call" | custom-call | tf_op jit(solution)/shard_map/place/pallas_call | solution.py:340

commit v5 on v4

--- a/solution.py
+++ b/solution.py
@@ -64,7 +64,7 @@
     others = far_first(ny, nz)[:-1]
     mine = z * ny + y
     near_columns = sorted(range(nz), key=lambda d: apart(d, nz))
-    halves = (near_columns[: nz // 2], near_columns[nz // 2 :])
+    halves = (near_columns[: nz - 2], near_columns[nz - 2 :])
 
     loads = [
         pltpu.make_async_copy(src, dst, load_sem.at[i])

time: 59.7 us -> 59.8 us (level)
  no operation moved by 1% of the time
where the time goes in v5:
time: 59.8 us; the launch traced here: 59.7 us
  Pallas kernels  59 us (99%)
  between operations  0.64 us (1%)
    pallas_call x1, Pallas kernels, local(): pl.pallas_call(functools.partial(kernel, sizes), out_shape=[pltpu.VMEM(s....  58 us

profile of v5, /device:TPU:1, one launch (start us, length us, event | category | flops | bytes accessed | tf_op | source)
XLA Modules:
  0.0 59.7 jit_solution(13558713530200308997)
XLA Ops:
  0.6 58.0 %layer.1 = (bf16[128,1024]{1,0:T(8,128)(2,1)S(1)}, bf16[128,1024]{1,0:T(8,128)(2,1)S(1)}, bf16[128,1024]{1,0:T(8,128)(2,1)S(1)}, bf16[128,1024]{1,0:T(8,128)(2,1)S(1)}, f32[2,1024]{1,0:T(2,128)S(1)}) custom-call(bf16[128,1024]{1,0:T(8,128)(2,1)} %bitcast.8, bf16[128,1024]{1,0:T(8,128)(2,1)} %bitcast.9, bf16[128,1024]{1,0:T(8,128)(2,1)} %bitcast.10, ...), custom_call_target="tpu_custom_call" | custom-call | tf_op jit(solution)/shard_map/layer/pallas_call | solution.py:310
  58.7 1.0 %place.1 = (bf16[128,1024]{1,0:T(8,128)(2,1)}, bf16[128,1024]{1,0:T(8,128)(2,1)}, bf16[128,1024]{1,0:T(8,128)(2,1)}, bf16[128,1024]{1,0:T(8,128)(2,1)}, f32[2,1024]{1,0:T(2,128)}) custom-call(bf16[128,1024]{1,0:T(8,128)(2,1)S(1)} %get-tuple-element.15.refs_0_, bf16[128,1024]{1,0:T(8,128)(2,1)S(1)} %get-tuple-element.16.refs_1_, ...), custom_call_target="tpu_custom_call" | custom-call | tf_op jit(solution)/shard_map/place/pallas_call | solution.py:340
